TPU v7x, 32 devices: a whole 2x2x4 slice. The times are simulated.
32 devices in a mesh: wide: 8 (over z, x), narrow: 4 (over y, core).
Axes of the slice: x: 2, y: 2, z: 4, core: 2. Of those that a mesh axis runs over, the one named last changes fastest.
Arguments:
- attn_heads: bfloat16 [1024, 1536], P('wide', 'narrow'), may hold values from -6 to 6
- w_out: bfloat16 [1536, 1536], P('narrow'), may hold values from -0.21875 to 0.21875
- residual: bfloat16 [1024, 1536], P('wide', 'narrow'), may hold values from -6 to 6
- norm_gain: float32 [1536], replicated, may hold values from 0.1 to 1.9
- route_ids: int32 [1024, 4], P('wide'), may hold values from 0 to 31, all different within a row; in each aligned block of 128 rows (0 to 127, 128 to 255, ...) at most 32 rows name the same one
- route_weight: float32 [1024, 4], P('wide'), may hold values from 0.1 to 1
- row_order: int32 [1024], P('wide'), may hold values from 0 to 1023, as said below
- slot_expert: int32 [64], replicated, may hold values from 0 to 31, as said below
- w_in: bfloat16 [64, 2, 768, 1536], P('wide', None, 'narrow')
- w_down: bfloat16 [64, 768, 1536], P('wide', 'narrow')
Outputs:
- block_out: bfloat16 [1024, 1536], P('wide', 'narrow')
Inputs may be any that keep to these rules, and one draw needn't show every extreme that they name: `route_ids`: each row names 4 different experts; among the 128 rows of one index of wide no expert is named more than 32 times. `row_order`: A permutation of the rows; of the 128 rows of each index of wide, exactly 16 have their initial position among the rows of each index of wide. `slot_expert`: every expert is held by one or more slots; slots holding the same expert hold equal w_in and w_down.
All inputs are finite; a program needn't handle non-finite values.
Results may differ from a plain program's by a relative error of at most 0.017.
Values may be sent and summed in bfloat16 or wider, within the bound.
A program may use at most 128 MiB of HBM per device.

v0:
```python
import jax
import jax.numpy as jnp
from jax import lax
from jax.sharding import PartitionSpec as P

EXPERTS = 32
CAP = 32


def running_rank(onehot):
    return jnp.sum((jnp.cumsum(onehot, axis=0) - onehot) * onehot, axis=1)


def local(
    attn_heads,
    w_out,
    residual,
    norm_gain,
    route_ids,
    route_weight,
    row_order,
    slot_expert,
    w_in,
    w_down,
):
    row_count = residual.shape[0]
    wide_count = lax.axis_size("wide")
    width_local = residual.shape[1]
    partial_terms = jnp.dot(attn_heads, w_out, preferred_element_type=jnp.float32)
    projected = lax.psum_scatter(
        partial_terms.astype(jnp.bfloat16), "narrow", scatter_dimension=1, tiled=True
    ).astype(jnp.float32)
    hidden = (residual.astype(jnp.float32) + projected).astype(jnp.bfloat16)
    whole_rows = lax.all_gather(hidden, "narrow", axis=1, tiled=True).astype(jnp.float32)
    mean_sq = jnp.mean(whole_rows * whole_rows, axis=1, keepdims=True)
    normed = (whole_rows * lax.rsqrt(mean_sq + 1e-06) * norm_gain).astype(jnp.bfloat16)
    slot_count = slot_expert.shape[0]
    slot_local = w_in.shape[0]
    top_count = route_ids.shape[1]
    model_width = normed.shape[1]
    held = (slot_expert[None, :] == jnp.arange(EXPERTS, dtype=jnp.int32)[:, None]).astype(jnp.int32)
    copies = jnp.sum(held, axis=1)
    replica_rank = jnp.cumsum(held, axis=1) - held
    flat_ids = route_ids.reshape(-1)
    choose_expert = (flat_ids[:, None] == jnp.arange(EXPERTS, dtype=jnp.int32)[None, :]).astype(
        jnp.int32
    )
    copy_count = jnp.sum(choose_expert * copies[None, :], axis=1)
    replica = jnp.repeat(row_order, top_count) % copy_count
    held_rows = jnp.sum(choose_expert[:, :, None] * held[None, :, :], axis=1)
    rank_rows = jnp.sum(choose_expert[:, :, None] * replica_rank[None, :, :], axis=1)
    slot_hit = held_rows * (rank_rows == replica[:, None]).astype(jnp.int32)
    slot_index = jnp.sum(slot_hit * jnp.arange(slot_count, dtype=jnp.int32)[None, :], axis=1)
    position = slot_index * CAP + running_rank(slot_hit)
    outgoing = (
        jnp.zeros((slot_count * CAP, model_width), jnp.bfloat16)
        .at[position]
        .set(jnp.repeat(normed, top_count, axis=0))
    )
    outgoing = outgoing.reshape(wide_count, slot_local, CAP, model_width)
    gate_up = jnp.einsum(
        "nscd,sghd->nscgh",
        lax.all_to_all(outgoing, "wide", split_axis=0, concat_axis=0, tiled=True),
        w_in,
        preferred_element_type=jnp.float32,
    )
    active = (jax.nn.relu(gate_up[:, :, :, 0, :]) * gate_up[:, :, :, 1, :]).astype(jnp.bfloat16)
    lowered = jnp.einsum("nsch,shd->nscd", active, w_down, preferred_element_type=jnp.float32)
    pieces = lowered.astype(jnp.bfloat16)
    summed = lax.psum_scatter(
        pieces.astype(jnp.float32).astype(jnp.bfloat16), "narrow", scatter_dimension=3, tiled=True
    )
    returned = lax.all_to_all(summed, "wide", split_axis=0, concat_axis=0, tiled=True)
    expert_out = returned.reshape(slot_count * CAP, width_local)[position]
    weighted = route_weight[:, :, None] * expert_out.reshape(
        row_count, top_count, width_local
    ).astype(jnp.float32)
    mixed = (hidden.astype(jnp.float32) + jnp.sum(weighted, axis=1)).astype(jnp.bfloat16)
    pair_rows = row_count // wide_count
    target_dev = row_order // row_count
    target_place = row_order % row_count
    choose_target = (
        target_dev[:, None] == jnp.arange(wide_count, dtype=jnp.int32)[None, :]
    ).astype(jnp.int32)
    packed_index = target_dev * pair_rows + running_rank(choose_target)
    packed = jnp.zeros((row_count, width_local), jnp.bfloat16).at[packed_index].set(mixed)
    places = jnp.zeros((row_count,), jnp.int32).at[packed_index].set(target_place)
    arrived_rows, arrived_places = (
        lax.all_to_all(
            packed.reshape(wide_count, pair_rows, width_local),
            "wide",
            split_axis=0,
            concat_axis=0,
            tiled=True,
        ),
        lax.all_to_all(
            places.reshape(wide_count, pair_rows), "wide", split_axis=0, concat_axis=0, tiled=True
        ),
    )
    return (
        jnp.zeros((row_count, width_local), jnp.bfloat16)
        .at[arrived_places.reshape(-1)]
        .set(arrived_rows.reshape(row_count, width_local))
    )


def solution(mesh):
    placed = (
        P("wide", "narrow"),
        P("narrow", None),
        P("wide", "narrow"),
        P(),
        P("wide", None),
        P("wide", None),
        P("wide"),
        P(),
        P("wide", None, "narrow", None),
        P("wide", "narrow", None),
    )
    return jax.shard_map(
        local, mesh=mesh, in_specs=placed, out_specs=P("wide", "narrow"), check_vma=False
    )
```

profile of v0, /device:TPU:0, one launch (start us, length us, event | category | flops | bytes accessed | tf_op | source)
XLA Modules:
  0.0 420.6 jit_solution(5437128707544489425)
XLA Ops:
  6.5 0.0 copy-start
  6.5 0.0 copy-start.3
  6.5 0.0 reduce-scatter.7.cloned.1.call-start
  6.5 1.3 copy-done
  7.8 1.3 convolution_convert_fusion
  9.1 0.9 copy.37
  10.0 0.0 reduce-scatter.7.cloned.1.call-update
  10.0 0.0 reduce-scatter.9.cloned.1.call-start
  10.1 0.7 fusion.25
  10.7 0.2 reduce_window_sum.38
  10.9 0.8 fusion.26
  11.7 0.8 copy.27
  12.5 0.1 eq.79
  12.6 0.1 select_reduce_fusion
  12.7 0.7 broadcast_in_dim.14
  13.4 0.1 reshape.213
  13.6 0.9 multiply_reduce_fusion.1
  14.5 0.1 add_select_fusion
  14.7 1.2 reduce-window.6
  15.9 0.2 slice_reduce_fusion
  16.1 0.1 multiply_reduce_fusion.3
  16.3 17.4 %reduce-scatter.7.cloned.1.call-done = bf16[384,128]{1,0:T(8,128)(2,1)} async-done(((bf16[1536,128]{1,0:T(8,128)(2,1)}), bf16[384,128]{1,0:T(8,128)(2,1)}) %reduce-scatter.7.cloned.1.call-update) | async-done | bytes 98320
  33.7 1.0 copy.38
  34.7 0.0 copy-done.2
  34.7 6.1 %all_gather.3 = bf16[128,1536]{1,0:T(8,128)(2,1)S(1)} all-gather(bf16[128,384]{1,0:T(8,128)(2,1)S(1)} %add_convert_fusion.1), channel_id=1, replica_groups=mesh['wide'=8,'narrow'=4] {'narrow'}, dimensions={1}, use_global_device_ids=true | all-gather | bytes 491520 | tf_op jit(solution)/shard_map/all_gather | solution.py:34
  40.9 0.2 fusion.15
  41.1 0.0 copy-done.3
  41.1 0.2 fusion.17
  41.2 0.4 broadcast_in_dim.16
  41.6 1.3 reshape.242
  43.0 7.7 %scatter_custom_fusion.1 = bf16[2048,1536]{1,0:T(8,128)(2,1)} fusion(s32[512]{0:T(512)S(1)} %bitcast.65, bf16[512,1536]{1,0:T(8,128)(2,1)} %reshape.242, bf16[]{:T(256)} %constant.53.clone.1), kind=kCustom, calls=%fused_computation.12 | custom fusion | bytes 6291968 | tf_op jit(solution)/shard_map/scatter | solution.py:58
  50.6 144.2 %all_to_all.24 = bf16[8,8,32,1536]{3,2,1,0:T(8,128)(2,1)} all-to-all(bf16[8,8,32,1536]{3,2,1,0:T(8,128)(2,1)} %bitcast.59), channel_id=1, replica_groups=mesh['wide'=8,'narrow'=4] {'wide'}, dimensions={0} | all-to-all | bytes 12582912 | tf_op jit(solution)/shard_map/all_to_all | solution.py:63
  194.9 10.9 %fusion.6 = f32[8,8,32,2,192]{4,2,3,0,1:T(8,128)} fusion(bf16[8,2,192,1536]{3,2,1,0:T(8,128)(2,1)} %param.18, bf16[8,8,32,1536]{3,2,1,0:T(8,128)(2,1)} %all_to_all.24), kind=kOutput, calls=%fused_computation.15 | convolution fusion | flops 2415919104 | bytes 18874368 | tf_op jit(solution)/shard_map/nscd,sghd->nscgh/dot_general | solution.py:61
  205.7 8.1 %convert_bitcast_fusion = bf16[8,8,32,1536]{3,2,0,1:T(8,128)(2,1)} fusion(bf16[8,192,1536]{2,1,0:T(8,128)(2,1)} %param.19, f32[8,8,32,2,192]{4,2,3,0,1:T(8,128)} %fusion.6), kind=kOutput, calls=%fused_computation.8 | convolution fusion | flops 1212284928 | bytes 14155776 | tf_op jit(solution)/shard_map/nsch,shd->nscd/dot_general | solution.py:68
  213.8 33.7 %copy.39 = bf16[8,8,32,1536]{2,0,1,3:T(8,128)(2,1)} copy(bf16[8,8,32,1536]{3,2,0,1:T(8,128)(2,1)} %convert_bitcast_fusion) | data formatting | bytes 12582912
  247.5 33.1 %reshape.269 = bf16[1536,2048]{1,0:T(8,128)(2,1)} reshape(bf16[1536,8,8,32]{3,2,1,0:T(8,128)(2,1)} %bitcast.58) | data formatting | bytes 12582912
  280.6 0.0 copy-start.5
  280.6 0.0 reduce-scatter.9.cloned.1.call-update
  280.6 0.6 copy-done.5
  281.3 0.1 fusion.21
  281.3 0.2 reduce_window_sum.37
  281.5 0.2 select_reduce_fusion.1
  281.7 1.0 scatter_custom_fusion
  282.7 0.7 all_to_all.15
  283.4 3.6 all-to-all-start
  287.0 50.6 %reduce-scatter.9.cloned.1.call-done = bf16[384,2048]{1,0:T(8,128)(2,1)} async-done(((bf16[1536,2048]{1,0:T(8,128)(2,1)}), bf16[384,2048]{1,0:T(8,128)(2,1)}) %reduce-scatter.9.cloned.1.call-update) | async-done | bytes 1572880
  337.6 8.4 %reshape.270 = bf16[384,8,8,32]{3,2,1,0:T(8,128)(2,1)} reshape(bf16[384,2048]{1,0:T(8,128)(2,1)} %reduce-scatter.9.cloned.1.call-done) | data formatting | bytes 3145728
  345.9 8.7 %copy.31 = bf16[8,8,32,384]{3,2,1,0:T(8,128)(2,1)} copy(bf16[8,8,32,384]{2,0,1,3:T(8,128)(2,1)} %bitcast.60) | data formatting | bytes 3145728 | tf_op jit(solution)/shard_map/reduce_scatter | solution.py:70
  354.6 0.0 all-to-all-done
  354.6 5.5 %all-to-all-start.2 = ((bf16[8,8,32,384]{3,2,1,0:T(8,128)(2,1)}), bf16[8,8,32,384]{3,2,1,0:T(8,128)(2,1)S(1)}, u32[]{:S(2)}, u32[]{:S(2)}) async-start(bf16[8,8,32,384]{3,2,1,0:T(8,128)(2,1)} %copy.31), calls=%async_computation.2 | async-start | bytes 3145728 | tf_op jit(solution)/shard_map/all_to_all | solution.py:73
  360.1 0.0 copy-done.4
  360.1 0.1 copy.26
  360.2 0.5 broadcast.210
  360.7 0.7 reduce.5
  361.4 0.1 reshape.212
  361.5 35.6 %all-to-all-done.2 = bf16[8,8,32,384]{3,2,1,0:T(8,128)(2,1)S(1)} async-done(((bf16[8,8,32,384]{3,2,1,0:T(8,128)(2,1)}), bf16[8,8,32,384]{3,2,1,0:T(8,128)(2,1)S(1)}, u32[]{:S(2)}, u32[]{:S(2)}) %all-to-all-start.2) | async-done | bytes 1572896 | tf_op jit(solution)/shard_map/all_to_all | solution.py:73
  397.1 1.9 gather_fusion
  399.0 0.2 reshape.221
  399.2 0.5 multiply_reduce_fusion.2
  399.8 1.6 scatter_custom_fusion.2
  401.4 3.6 all-to-all-start.3
  405.1 7.1 %all-to-all-done.3 = bf16[8,16,384]{2,1,0:T(8,128)(2,1)S(1)} async-done(((bf16[8,16,384]{2,1,0:T(8,128)(2,1)}), bf16[8,16,384]{2,1,0:T(8,128)(2,1)S(1)}, u32[]{:S(2)}, u32[]{:S(2)}) %all-to-all-start.3) | async-done | bytes 98336 | tf_op jit(solution)/shard_map/all_to_all | solution.py:89
  412.2 1.6 scatter_custom_fusion.3
  413.8 0.0 copy-done.1
  (16 shorter events, 0.2 us)
Async XLA Ops:
  6.5 1.3 copy-start
  6.5 28.2 %copy-start.2 = (bf16[128,384]{1,0:T(8,128)(2,1)S(1)}, bf16[128,384]{1,0:T(8,128)(2,1)}, u32[]{:S(2)}) copy-start(bf16[128,384]{1,0:T(8,128)(2,1)} %param.12) | copy-start | bytes 294916
  6.5 34.5 %copy-start.3 = (f32[1536]{0:T(1024)S(1)}, f32[1536]{0:T(1024)}, u32[]{:S(2)}) copy-start(f32[1536]{0:T(1024)} %param.13) | copy-start | bytes 18436
  6.5 27.1 %reduce-scatter.7.cloned.1.call-start = ((), (), s32[]{:S(2)}) async-start(), calls=%async_computation.6 | async-start | bytes 491520
  10.0 327.6 %reduce-scatter.9.cloned.1.call-start = ((), (), s32[]{:S(2)}) async-start(), calls=%async_computation.7 | async-start | bytes 7864320
  280.6 0.7 copy-start.5
  283.4 71.2 %all-to-all-start = ((s32[8,1,16]{2,1,0:T(1,128)}), s32[8,1,16]{2,1,0:T(1,128)S(1)}, u32[]{:S(2)}, u32[]{:S(2)}) async-start(s32[8,1,16]{2,1,0:T(1,128)} %bitcast), calls=%async_computation | async-start | bytes 8192 | tf_op jit(solution)/shard_map/all_to_all | solution.py:96
  345.9 14.2 %copy-start.4 = (f32[128,4]{0,1:T(4,128)S(1)}, f32[128,4]{0,1:T(4,128)}, u32[]{:S(2)}) copy-start(f32[128,4]{0,1:T(4,128)} %param.15) | copy-start | bytes 6148
  345.9 67.9 %copy-start.1 = (bf16[384,1536]{1,0:T(8,128)(2,1)S(1)}, bf16[384,1536]{1,0:T(8,128)(2,1)}, u32[]{:S(2)}) copy-start(bf16[384,1536]{1,0:T(8,128)(2,1)} %param.11) | copy-start | bytes 3538948
  354.6 42.5 %all-to-all-start.2 = ((bf16[8,8,32,384]{3,2,1,0:T(8,128)(2,1)}), bf16[8,8,32,384]{3,2,1,0:T(8,128)(2,1)S(1)}, u32[]{:S(2)}, u32[]{:S(2)}) async-start(bf16[8,8,32,384]{3,2,1,0:T(8,128)(2,1)} %copy.31), calls=%async_computation.2 | async-start | bytes 3145728 | tf_op jit(solution)/shard_map/all_to_all | solution.py:73
  401.4 10.8 %all-to-all-start.3 = ((bf16[8,16,384]{2,1,0:T(8,128)(2,1)}), bf16[8,16,384]{2,1,0:T(8,128)(2,1)S(1)}, u32[]{:S(2)}, u32[]{:S(2)}) async-start(bf16[8,16,384]{2,1,0:T(8,128)(2,1)} %bitcast.16), calls=%async_computation.3 | async-start | bytes 196608 | tf_op jit(solution)/shard_map/all_to_all | solution.py:89
Sparse Core Ops, SparseCore 0:
  10.1 23.5 reduce-scatter.6
  280.7 56.7 reduce-scatter.8
where the time goes:
time: 422 us; the launch traced here: 421 us
  blocking collectives  150 us (36%)
  waiting for transfers between devices  111 us (26%)
  local copies, waits for them, and re-layouts  105 us (25%)
  matrix products  20.2 us (5%)
  between operations  13.6 us (3%)
  starting transfers between devices  12.8 us (3%)
  other arithmetic  7.84 us (2%)
    all_to_all x1, blocking collectives, local(): lax.all_to_all(outgoing, 'wide', split_axis=0, concat_axis=0, tiled=True)  144 us
    unnamed x19, local copies, waits for them, and re-layouts  79.9 us
    unnamed x4, waiting for transfers between devices  68 us
    all_to_all x1, waiting for transfers between devices, local(): lax.all_to_all(summed, 'wide', split_axis=0, concat_axis=0, tiled=True)  35.6 us
    dot_general x1, matrix products, local(): jnp.einsum('nscd,sghd->nscgh', lax.all_to_all(outgoing, 'wide', split_axi...  10.9 us
    reduce_scatter x1, local copies, waits for them, and re-layouts, local(): lax.psum_scatter(pieces.astype(jnp.float32).astype(jnp.bfloat16), 'narrow...  8.66 us
  transfers between devices with their start and end apart: 5, of which 4 were waited for; matrix products, arithmetic and copies ran while one was open for 6% of the time, Pallas kernels for 0%

commit v1 on v0

v1 whole, which is shorter than its diff:
```python
import jax
import jax.numpy as jnp
from jax import lax
from jax.sharding import PartitionSpec as P


def local(
    attn_heads,
    w_out,
    residual,
    norm_gain,
    route_ids,
    route_weight,
    row_order,
    slot_expert,
    w_in,
    w_down,
):
    rows = residual.shape[0]
    wide = lax.axis_size("wide")
    me = lax.axis_index("wide")
    width_local = residual.shape[1]
    slot_local, _, hid, width = w_in.shape
    pair = rows // wide

    target = row_order // rows
    earlier = jnp.arange(rows)[None, :] < jnp.arange(rows)[:, None]
    rank = jnp.sum((target[:, None] == target[None, :]) & earlier, axis=1, dtype=jnp.int32)
    packed = target * pair + rank
    perm = packed[None, :] == jnp.arange(rows, dtype=jnp.int32)[:, None]
    order = perm.astype(jnp.bfloat16)
    meta = jnp.concatenate(
        [
            route_ids.astype(jnp.float32),
            route_weight,
            (row_order % rows).astype(jnp.float32)[:, None],
        ],
        axis=1,
    )
    meta = jnp.sum(jnp.where(perm[:, :, None], meta[None], 0.0), axis=1)
    metas = lax.all_gather(meta, "wide", axis=0, tiled=True)
    attn = jnp.dot(order, attn_heads, preferred_element_type=jnp.float32).astype(jnp.bfloat16)
    res = jnp.dot(order, residual, preferred_element_type=jnp.float32)

    partial_terms = jnp.dot(attn, w_out, preferred_element_type=jnp.float32)
    projected = lax.psum_scatter(
        partial_terms.astype(jnp.bfloat16), "narrow", scatter_dimension=1, tiled=True
    ).astype(jnp.float32)
    hidden = (res + projected).astype(jnp.bfloat16)
    column = lax.all_gather(hidden, "wide", axis=0, tiled=True)

    def regroup(x):
        return (
            x.reshape(wide, wide, pair, x.shape[1])
            .transpose(1, 0, 2, 3)
            .reshape(wide * rows, x.shape[1])
        )

    column = regroup(column)
    metas = regroup(metas)
    whole = lax.all_gather(column, "narrow", axis=1, tiled=True).astype(jnp.float32)
    mean_sq = jnp.mean(whole * whole, axis=1, keepdims=True)
    normed = (whole * lax.rsqrt(mean_sq + 1e-06) * norm_gain).astype(jnp.bfloat16)

    slots = slot_expert.shape[0]
    before = jnp.arange(slots)[None, :] < jnp.arange(slots)[:, None]
    repeated = jnp.any((slot_expert[:, None] == slot_expert[None, :]) & before, axis=1)
    used = jnp.where(repeated, -1, slot_expert)
    mine = lax.dynamic_slice_in_dim(used, me * slot_local, slot_local).astype(jnp.float32)
    ids, weights, places = metas[:, :4], metas[:, 4:8], metas[:, 8]
    coef = jnp.sum(
        jnp.where(ids[:, :, None] == mine[None, None, :], weights[:, :, None], 0.0), axis=1
    )

    gate = jnp.einsum("rd,shd->rsh", normed, w_in[:, 0], preferred_element_type=jnp.float32)
    up = jnp.einsum("rd,shd->rsh", normed, w_in[:, 1], preferred_element_type=jnp.float32)
    act = (jax.nn.relu(gate) * up * coef[:, :, None]).astype(jnp.bfloat16)
    lowered = jnp.dot(
        act.reshape(wide * rows, slot_local * hid),
        w_down.reshape(slot_local * hid, width),
        preferred_element_type=jnp.float32,
    ).astype(jnp.bfloat16)
    summed = lax.psum_scatter(lowered, "narrow", scatter_dimension=1, tiled=True)
    mixed = lax.psum_scatter(summed, "wide", scatter_dimension=0, tiled=True)
    base = lax.dynamic_slice_in_dim(column, me * rows, rows)
    mixed = (base.astype(jnp.float32) + mixed.astype(jnp.float32)).astype(jnp.bfloat16)
    place = lax.dynamic_slice_in_dim(places, me * rows, rows).astype(jnp.int32)
    back = (place[None, :] == jnp.arange(rows, dtype=jnp.int32)[:, None]).astype(jnp.bfloat16)
    return jnp.dot(back, mixed, preferred_element_type=jnp.float32).astype(jnp.bfloat16)


def solution(mesh):
    placed = (
        P("wide", "narrow"),
        P("narrow", None),
        P("wide", "narrow"),
        P(),
        P("wide", None),
        P("wide", None),
        P("wide"),
        P(),
        P("wide", None, "narrow", None),
        P("wide", "narrow", None),
    )
    return jax.shard_map(
        local, mesh=mesh, in_specs=placed, out_specs=P("wide", "narrow"), check_vma=False
    )
```

time: 422 us -> 248 us (0.59)
  local copies, waits for them, and re-layouts: 105 us -> 10.5 us
  blocking collectives: 150 us -> 62.6 us
  waiting for transfers between devices: 111 us -> 125 us
  starting transfers between devices: 12.8 us -> 0.16 us
  matrix products: 20.2 us -> 31.8 us
    all_to_all x1 -> x0, blocking collectives: 144 us -> none  [local(): lax.all_to_all(outgoing, 'wide', split_axis=0, concat_axis=0, tiled=True)]
    unnamed x19 -> x14, local copies, waits for them, and re-layouts: 79.9 us -> 9.15 us
    reduce_scatter x0 -> x1, waiting for transfers between devices: none -> 63.6 us  [local(): mixed = lax.psum_scatter(summed, 'wide', scatter_dimension=0, tiled=True)]
    all_gather x1 -> x2, blocking collectives: 6.15 us -> 62.6 us  [the longest x1 32 us: local(): column = lax.all_gather(hidden, 'wide', axis=0, tiled=True)]
    all_to_all x3 -> x0, waiting for transfers between devices: 42.7 us -> none  [the longest x1 35.6 us: local(): lax.all_to_all(summed, 'wide', split_axis=0, concat_axis=0, tiled=True)]
    all_to_all x3 -> x0, starting transfers between devices: 12.8 us -> none  [the longest x1 5.51 us: local(): lax.all_to_all(summed, 'wide', split_axis=0, concat_axis=0, tiled=True)]
    dot_general x3 -> x5, matrix products: 20.2 us -> 31.8 us  [the longest x1 17.3 us: local(): jnp.dot(act.reshape(wide * rows, slot_local * hid), w_down.reshape(slot_l...]
    scatter x3 -> x0, local copies, waits for them, and re-layouts: 10.3 us -> none  [the longest x1 7.66 us: local(): outgoing = jnp.zeros((slot_count * CAP, model_width), jnp.bfloat16).at[po...]
  transfers between devices with their start and end apart: 5 -> 4, of which waited for: 4 -> 3; matrix products, arithmetic and copies ran while one was open for 6% -> 0% of each run, Pallas kernels for 0% -> 0%
where the time goes in v1:
time: 248 us
  waiting for transfers between devices  125 us (50%)
  blocking collectives  62.6 us (25%)
  matrix products  31.8 us (13%)
  between operations  13.3 us (5%)
  local copies, waits for them, and re-layouts  10.5 us (4%)
  other arithmetic  4.13 us (2%)
    reduce_scatter x1, waiting for transfers between devices, local(): mixed = lax.psum_scatter(summed, 'wide', scatter_dimension=0, tiled=True)  63.6 us
    unnamed x6, waiting for transfers between devices  61.8 us
    all_gather x1, blocking collectives, local(): column = lax.all_gather(hidden, 'wide', axis=0, tiled=True)  32 us
    all_gather x1, blocking collectives, local(): metas = lax.all_gather(meta, 'wide', axis=0, tiled=True)  30.5 us
    dot_general x1, matrix products, local(): jnp.dot(act.reshape(wide * rows, slot_local * hid), w_down.reshape(slot_l...  17.3 us
    dot_general x1, matrix products, local(): jnp.einsum('rd,shd->rsh', normed, w_in[:, 1], preferred_element_type=jnp....  10.3 us
    unnamed x14, local copies, waits for them, and re-layouts  9.15 us
  transfers between devices with their start and end apart: 4, of which 3 were waited for; matrix products, arithmetic and copies ran while one was open for 0% of the time, Pallas kernels for 0%

profile of v1, /device:TPU:0, one launch (start us, length us, event | category | flops | bytes accessed | tf_op | source)
XLA Modules:
  0.0 247.9 jit_solution(12075540634487245164)
XLA Ops:
  6.5 0.0 copy-start
  6.5 0.0 copy-start.2
  6.5 0.0 copy-start.1
  6.5 0.0 copy-start.4
  6.5 0.0 copy-start.3
  6.5 0.0 reduce-scatter.10.cloned.1.call-start
  6.6 0.8 fusion.29
  7.3 0.2 convert_reduce_fusion
  7.5 0.3 copy-done
  7.8 1.4 convolution_convert_fusion
  9.2 0.9 copy.36
  10.1 0.0 reduce-scatter.10.cloned.1.call-update
  10.1 0.0 all-gather.2.cloned.1.call-start
  10.2 23.6 %reduce-scatter.10.cloned.1.call-done = bf16[384,128]{1,0:T(8,128)(2,1)} async-done(((bf16[1536,128]{1,0:T(8,128)(2,1)}), bf16[384,128]{1,0:T(8,128)(2,1)}) %reduce-scatter.10.cloned.1.call-update) | async-done | bytes 98320
  33.8 1.0 copy.37
  34.8 1.1 fusion.19
  35.9 32.0 %all_gather.10 = bf16[1024,384]{1,0:T(8,128)(2,1)S(1)} all-gather(bf16[128,384]{1,0:T(8,128)(2,1)S(1)} %fusion.19), channel_id=1, replica_groups=mesh['wide'=8,'narrow'=4] {'wide'}, dimensions={0}, use_global_device_ids=true | all-gather | bytes 884736 | tf_op jit(solution)/shard_map/all_gather | solution.py:50
  67.9 1.0 copy.33
  68.9 0.0 all-gather.2.cloned.1.call-update
  69.0 0.0 reduce-scatter.12.cloned.1.call-start
  69.0 0.0 copy-done.2
  69.0 0.0 copy-done.1
  69.1 0.2 select_reduce_fusion
  69.3 30.5 %all_gather.9 = f32[1024,9]{0,1:T(8,128)S(1)} all-gather(f32[128,9]{0,1:T(8,128)S(1)} %select_reduce_fusion), channel_id=1, replica_groups=mesh['wide'=8,'narrow'=4] {'wide'}, dimensions={0}, use_global_device_ids=true | all-gather | bytes 41472 | tf_op jit(solution)/shard_map/all_gather | solution.py:41
  99.8 0.1 reshape.57
  100.0 0.1 copy.32
  100.0 0.2 reshape.58
  100.2 0.0 copy-done.4
  100.2 0.2 fusion.27
  100.4 0.1 dynamic-slice_convert_fusion
  100.5 0.1 select_reduce_fusion.1
  100.6 0.0 all-gather.2.cloned.1.call-done
  100.6 2.6 %fusion = f32[1024]{0:T(1024)S(1)} fusion(bf16[1024,1536]{1,0:T(8,128)(2,1)} %all-gather.2.cloned.1.call-done), kind=kLoop, calls=%fused_computation.2 | loop fusion | flops 4717568 | bytes 3149824 | tf_op jit(solution)/shard_map/reduce_sum | solution.py:62
  103.2 0.0 copy-done.3
  103.2 10.3 %fusion.3 = f32[1024,8,192]{0,2,1:T(8,128)} fusion(bf16[8,2,192,1536]{3,2,1,0:T(8,128)(2,1)} %param.18, bf16[1024,1536]{1,0:T(8,128)(2,1)} %all-gather.2.cloned.1.call-done, f32[1536]{0:T(1024)S(1)} %copy-done.3, f32[1024]{0:T(1024)S(1)} %add_rsqrt_fusion), kind=kOutput, calls=%fused_computation.7 | convolution fusion | flops 4838129664 | bytes 14166016 | tf_op jit(solution)/shard_map/rd,shd->rsh/dot_general | solution.py:76
  113.5 17.3 %bitcast_convert_fusion = bf16[1024,1536]{1,0:T(8,128)(2,1)} fusion(bf16[8,192,1536]{2,1,0:T(8,128)(2,1)} %param.19, f32[1024,8,192]{0,2,1:T(8,128)} %fusion.3, bf16[8,2,192,1536]{3,2,1,0:T(8,128)(2,1)} %param.18, f32[1024,8]{0,1:T(8,128)S(1)} %select_reduce_fusion.1, bf16[1024,1536]{1,0:T(8,128)(2,1)} %all-gather.2.cloned.1.call-done, ...), kind=kOutput, calls=%fused_computation.5 | convolution fusion | flops 9677832192 | bytes 22063104 | tf_op jit(solution)/shard_map/dot_general | solution.py:78
  130.8 4.6 %copy.38 = bf16[1024,1536]{0,1:T(8,128)(2,1)} copy(bf16[1024,1536]{1,0:T(8,128)(2,1)} %bitcast_convert_fusion) | data formatting | bytes 6291456
  135.5 0.0 reduce-scatter.12.cloned.1.call-update
  135.5 0.0 reduce-scatter.8.cloned.1.call-start
  135.6 38.1 %reduce-scatter.12.cloned.1.call-done = bf16[384,1024]{1,0:T(8,128)(2,1)} async-done(((bf16[1536,1024]{1,0:T(8,128)(2,1)}), bf16[384,1024]{1,0:T(8,128)(2,1)}) %reduce-scatter.12.cloned.1.call-update) | async-done | bytes 786448
  173.7 2.3 copy.39
  176.0 0.0 reduce-scatter.8.cloned.1.call-update
  176.0 63.6 %reduce-scatter.8.cloned.1.call-done = bf16[128,384]{1,0:T(8,128)(2,1)} async-done(((bf16[1024,384]{1,0:T(8,128)(2,1)}), bf16[128,384]{1,0:T(8,128)(2,1)}) %reduce-scatter.8.cloned.1.call-update) | async-done | bytes 98320 | tf_op jit(solution)/shard_map/reduce_scatter | solution.py:84
  239.6 1.8 convolution_convert_fusion.1
  (9 shorter events, 0.1 us)
Async XLA Ops:
  6.5 1.3 copy-start
  6.5 62.5 %copy-start.2 = (s32[128,4]{0,1:T(4,128)S(1)}, s32[128,4]{0,1:T(4,128)}, u32[]{:S(2)}) copy-start(s32[128,4]{0,1:T(4,128)} %param.14) | copy-start | bytes 6148
  6.5 62.5 %copy-start.1 = (f32[128,4]{0,1:T(4,128)S(1)}, f32[128,4]{0,1:T(4,128)}, u32[]{:S(2)}) copy-start(f32[128,4]{0,1:T(4,128)} %param.15) | copy-start | bytes 6148
  6.5 93.7 %copy-start.4 = (s32[64]{0:T(128)S(1)}, s32[64]{0:T(128)}, u32[]{:S(2)}) copy-start(s32[64]{0:T(128)} %param.17) | copy-start | bytes 772
  6.5 96.7 %copy-start.3 = (f32[1536]{0:T(1024)S(1)}, f32[1536]{0:T(1024)}, u32[]{:S(2)}) copy-start(f32[1536]{0:T(1024)} %param.13) | copy-start | bytes 18436
  6.5 27.3 %reduce-scatter.10.cloned.1.call-start = ((), (), s32[]{:S(2)}) async-start(), calls=%async_computation.5 | async-start | bytes 491520
  10.1 90.5 %all-gather.2.cloned.1.call-start = ((), (), s32[]{:S(2)}) async-start(), calls=%async_computation.3 | async-start | bytes 3932160 | tf_op jit(solution)/shard_map/all_gather | solution.py:61
  69.0 104.7 %reduce-scatter.12.cloned.1.call-start = ((), (), s32[]{:S(2)}) async-start(), calls=%async_computation.6 | async-start | bytes 3932160
  135.5 104.1 %reduce-scatter.8.cloned.1.call-start = ((), (), s32[]{:S(2)}) async-start(), calls=%async_computation.4 | async-start | bytes 884736 | tf_op jit(solution)/shard_map/reduce_scatter | solution.py:84
Sparse Core Ops, SparseCore 0:
  10.2 23.5 reduce-scatter.9
  69.1 28.5 all-gather.1
  135.6 38.0 reduce-scatter.11
  177.2 62.3 reduce-scatter.7

commit v2 on v1

--- a/solution.py
+++ b/solution.py
@@ -1,7 +1,313 @@
+import functools
+
 import jax
 import jax.numpy as jnp
 from jax import lax
+from jax.experimental import pallas as pl
+from jax.experimental.pallas import tpu as pltpu
 from jax.sharding import PartitionSpec as P
+
+MESH = pl.DeviceIdType.MESH
+NARROW = 4
+
+
+def remote(src, dst, send_sem, recv_sem, wide_index, narrow_index):
+    return pltpu.make_async_remote_copy(
+        src_ref=src,
+        dst_ref=dst,
+        send_sem=send_sem,
+        recv_sem=recv_sem,
+        device_id=(wide_index, narrow_index),
+        device_id_type=MESH,
+    )
+
+
+def greet(wide, me, col, others):
+    barrier = pltpu.get_barrier_semaphore()
+
+    def hello(j, carry):
+        pl.semaphore_signal(
+            barrier, inc=1, device_id=(lax.rem(me + j, wide), col), device_id_type=MESH
+        )
+        return carry
+
+    lax.fori_loop(1, wide, hello, 0)
+    for other in others:
+        pl.semaphore_signal(barrier, inc=1, device_id=(me, other), device_id_type=MESH)
+    pl.semaphore_wait(barrier, wide - 1 + len(others))
+
+
+def gather_kernel(
+    wide,
+    attn_ref,
+    w_ref,
+    res_ref,
+    out_ref,
+    parts,
+    got,
+    mine,
+    sum_send,
+    sum_recv,
+    local_sem,
+    wide_send,
+    wide_recv,
+    y_send,
+    y_recv,
+    core_send,
+    core_recv,
+):
+    me, col = lax.axis_index("wide"), lax.axis_index("narrow")
+    half, core = col // 2, lax.rem(col, 2)
+    y_col = (1 - half) * 2 + core
+    core_col = half * 2 + 1 - core
+    rows, cols = res_ref.shape
+    greet(wide, me, col, [lax.rem(col + k, NARROW) for k in range(1, NARROW)])
+
+    for p in range(NARROW):
+        parts[p] = jnp.dot(
+            attn_ref[...], w_ref[:, p * cols : (p + 1) * cols], preferred_element_type=jnp.float32
+        ).astype(jnp.bfloat16)
+    sums = []
+    for k in range(1, NARROW):
+        other = lax.rem(col + k, NARROW)
+        copy = remote(
+            parts.at[other], got.at[k - 1], sum_send.at[k - 1], sum_recv.at[k - 1], me, other
+        )
+        copy.start()
+        sums.append(copy)
+    total = res_ref[...] + parts[col].astype(jnp.float32)
+    for k, copy in enumerate(sums):
+        copy.wait_recv()
+        total += got[k].astype(jnp.float32)
+    mine[...] = total.astype(jnp.bfloat16)
+
+    def block(source, column):
+        return out_ref.at[
+            pl.ds(pl.multiple_of(source * rows, rows), rows),
+            pl.ds(pl.multiple_of(column * cols, cols), cols),
+        ]
+
+    def wide_copy(j):
+        return remote(
+            mine, block(me, col), wide_send.at[j], wide_recv.at[j], lax.rem(me + j, wide), col
+        )
+
+    def y_copy(j):
+        b = block(lax.rem(me - j + wide, wide), col)
+        return remote(b, b, y_send.at[j], y_recv.at[j], me, y_col)
+
+    def core_copy(j, h):
+        b = block(lax.rem(me - j + wide, wide), y_col if h else col)
+        return remote(b, b, core_send.at[h, j], core_recv.at[h, j], me, core_col)
+
+    def send_wide(j, carry):
+        wide_copy(j).start()
+        return carry
+
+    lax.fori_loop(1, wide, send_wide, 0)
+    keep = pltpu.make_async_copy(mine, block(me, col), local_sem)
+    keep.start()
+    keep.wait()
+    y_copy(0).start()
+    core_copy(0, 0).start()
+
+    def forward(j, carry):
+        wide_copy(j).wait_recv()
+        y_copy(j).start()
+        core_copy(j, 0).start()
+        y_copy(j - 1).wait_recv()
+        core_copy(j - 1, 1).start()
+        return carry
+
+    lax.fori_loop(1, wide, forward, 0)
+    y_copy(wide - 1).wait_recv()
+    core_copy(wide - 1, 1).start()
+
+    def finish(j, carry):
+        core_copy(j, 0).wait()
+        core_copy(j, 1).wait()
+        y_copy(j).wait_send()
+        return carry
+
+    lax.fori_loop(0, wide, finish, 0)
+
+    def finish_wide(j, carry):
+        wide_copy(j).wait_send()
+        return carry
+
+    lax.fori_loop(1, wide, finish_wide, 0)
+    for copy in sums:
+        copy.wait_send()
+
+
+def gather_call(attn, w_out, res, wide):
+    rows, cols = res.shape
+    dma = pltpu.SemaphoreType.DMA
+    vmem = pl.BlockSpec(memory_space=pltpu.VMEM)
+    return pl.pallas_call(
+        functools.partial(gather_kernel, wide),
+        out_shape=jax.ShapeDtypeStruct((wide * rows, NARROW * cols), jnp.bfloat16),
+        in_specs=[vmem] * 3,
+        out_specs=pl.BlockSpec(memory_space=pl.ANY),
+        scratch_shapes=[
+            pltpu.VMEM((NARROW, rows, cols), jnp.bfloat16),
+            pltpu.VMEM((NARROW - 1, rows, cols), jnp.bfloat16),
+            pltpu.VMEM((rows, cols), jnp.bfloat16),
+            dma((NARROW - 1,)),
+            dma((NARROW - 1,)),
+            dma,
+            dma((wide,)),
+            dma((wide,)),
+            dma((wide,)),
+            dma((wide,)),
+            dma((2, wide)),
+            dma((2, wide)),
+        ],
+        compiler_params=pltpu.CompilerParams(
+            collective_id=0, has_side_effects=True, vmem_limit_bytes=32 * 2**20
+        ),
+    )(attn, w_out, res)
+
+
+def scatter_kernel(
+    wide,
+    low_ref,
+    base_ref,
+    back_ref,
+    out_ref,
+    own,
+    core_got,
+    y_got,
+    wide_got,
+    local_sem,
+    core_send,
+    core_recv,
+    y_send,
+    y_recv,
+    wide_send,
+    wide_recv,
+):
+    me, col = lax.axis_index("wide"), lax.axis_index("narrow")
+    half, core = col // 2, lax.rem(col, 2)
+    y_col = (1 - half) * 2 + core
+    core_col = half * 2 + 1 - core
+    rows, cols = base_ref.shape
+    greet(wide, me, col, [y_col, core_col])
+
+    def target(j):
+        return lax.rem(me + 1 + j, wide)
+
+    def block(j, column):
+        return low_ref.at[
+            pl.ds(pl.multiple_of(target(j) * rows, rows), rows),
+            pl.ds(pl.multiple_of(column * cols, cols), cols),
+        ]
+
+    def core_copy(j, h):
+        return remote(
+            block(j, h * 2 + 1 - core),
+            core_got.at[j, h],
+            core_send.at[h, j],
+            core_recv.at[h, j],
+            me,
+            core_col,
+        )
+
+    def load(j, h):
+        return pltpu.make_async_copy(block(j, h * 2 + core), own.at[j, h], local_sem.at[h, j])
+
+    def y_copy(j):
+        return remote(own.at[j, 1 - half], y_got.at[j], y_send.at[j], y_recv.at[j], me, y_col)
+
+    def wide_copy(j):
+        return remote(
+            own.at[j, half], wide_got.at[j], wide_send.at[j], wide_recv.at[j], target(j), col
+        )
+
+    def begin(j, carry):
+        for h in range(2):
+            core_copy(j, h).start()
+            load(j, h).start()
+        return carry
+
+    lax.fori_loop(0, wide, begin, 0)
+
+    def add_core(j):
+        for h in range(2):
+            load(j, h).wait()
+            core_copy(j, h).wait_recv()
+            own[j, h] = (
+                own[j, h].astype(jnp.float32) + core_got[j, h].astype(jnp.float32)
+            ).astype(jnp.bfloat16)
+        y_copy(j).start()
+
+    def add_y(j):
+        y_copy(j).wait_recv()
+        return own[j, half].astype(jnp.float32) + y_got[j].astype(jnp.float32)
+
+    add_core(0)
+
+    def step(j, carry):
+        add_core(j)
+        own[j - 1, half] = add_y(j - 1).astype(jnp.bfloat16)
+        wide_copy(j - 1).start()
+        return carry
+
+    lax.fori_loop(1, wide, step, 0)
+    total = add_y(wide - 1)
+
+    def collect(j, acc):
+        wide_copy(j).wait_recv()
+        return acc + wide_got[j].astype(jnp.float32)
+
+    total = lax.fori_loop(0, wide - 1, collect, total)
+    mixed = (base_ref[...].astype(jnp.float32) + total).astype(jnp.bfloat16)
+    out_ref[...] = jnp.dot(back_ref[...], mixed, preferred_element_type=jnp.float32).astype(
+        jnp.bfloat16
+    )
+
+    def finish(j, carry):
+        core_copy(j, 0).wait_send()
+        core_copy(j, 1).wait_send()
+        y_copy(j).wait_send()
+        return carry
+
+    lax.fori_loop(0, wide, finish, 0)
+
+    def finish_wide(j, carry):
+        wide_copy(j).wait_send()
+        return carry
+
+    lax.fori_loop(0, wide - 1, finish_wide, 0)
+
+
+def scatter_call(low, base, back, wide):
+    rows, cols = base.shape
+    dma = pltpu.SemaphoreType.DMA
+    vmem = pl.BlockSpec(memory_space=pltpu.VMEM)
+    scratch = 6 * wide * rows * cols * 2
+    return pl.pallas_call(
+        functools.partial(scatter_kernel, wide),
+        out_shape=jax.ShapeDtypeStruct((rows, cols), jnp.bfloat16),
+        in_specs=[pl.BlockSpec(memory_space=pl.ANY), vmem, vmem],
+        out_specs=vmem,
+        scratch_shapes=[
+            pltpu.VMEM((wide, 2, rows, cols), jnp.bfloat16),
+            pltpu.VMEM((wide, 2, rows, cols), jnp.bfloat16),
+            pltpu.VMEM((wide, rows, cols), jnp.bfloat16),
+            pltpu.VMEM((wide, rows, cols), jnp.bfloat16),
+            dma((2, wide)),
+            dma((2, wide)),
+            dma((2, wide)),
+            dma((wide,)),
+            dma((wide,)),
+            dma((wide,)),
+            dma((wide,)),
+        ],
+        compiler_params=pltpu.CompilerParams(
+            collective_id=1, has_side_effects=True, vmem_limit_bytes=scratch + 12 * 2**20
+        ),
+    )(low, base, back)
 
 
 def local(
@@ -42,13 +348,6 @@
     attn = jnp.dot(order, attn_heads, preferred_element_type=jnp.float32).astype(jnp.bfloat16)
     res = jnp.dot(order, residual, preferred_element_type=jnp.float32)
 
-    partial_terms = jnp.dot(attn, w_out, preferred_element_type=jnp.float32)
-    projected = lax.psum_scatter(
-        partial_terms.astype(jnp.bfloat16), "narrow", scatter_dimension=1, tiled=True
-    ).astype(jnp.float32)
-    hidden = (res + projected).astype(jnp.bfloat16)
-    column = lax.all_gather(hidden, "wide", axis=0, tiled=True)
-
     def regroup(x):
         return (
             x.reshape(wide, wide, pair, x.shape[1])
@@ -56,9 +355,9 @@
             .reshape(wide * rows, x.shape[1])
         )
 
-    column = regroup(column)
+    gathered = regroup(gather_call(attn, w_out, res, wide))
     metas = regroup(metas)
-    whole = lax.all_gather(column, "narrow", axis=1, tiled=True).astype(jnp.float32)
+    whole = gathered.astype(jnp.float32)
     mean_sq = jnp.mean(whole * whole, axis=1, keepdims=True)
     normed = (whole * lax.rsqrt(mean_sq + 1e-06) * norm_gain).astype(jnp.bfloat16)
 
@@ -80,13 +379,14 @@
         w_down.reshape(slot_local * hid, width),
         preferred_element_type=jnp.float32,
     ).astype(jnp.bfloat16)
-    summed = lax.psum_scatter(lowered, "narrow", scatter_dimension=1, tiled=True)
-    mixed = lax.psum_scatter(summed, "wide", scatter_dimension=0, tiled=True)
-    base = lax.dynamic_slice_in_dim(column, me * rows, rows)
-    mixed = (base.astype(jnp.float32) + mixed.astype(jnp.float32)).astype(jnp.bfloat16)
+    base = lax.dynamic_slice(
+        gathered,
+        (me * rows, lax.axis_index("narrow") * width_local),
+        (rows, width_local),
+    )
     place = lax.dynamic_slice_in_dim(places, me * rows, rows).astype(jnp.int32)
     back = (place[None, :] == jnp.arange(rows, dtype=jnp.int32)[:, None]).astype(jnp.bfloat16)
-    return jnp.dot(back, mixed, preferred_element_type=jnp.float32).astype(jnp.bfloat16)
+    return scatter_call(lowered, base, back, wide)
 
 
 def solution(mesh):

time: 248 us -> 134 us (0.54)
  waiting for transfers between devices: 125 us -> 0 us
  Pallas kernels: 0 us -> 67.1 us
  blocking collectives: 62.6 us -> 32.3 us
  between operations: 13.3 us -> 0.19 us
  matrix products: 31.8 us -> 24.9 us
  local copies, waits for them, and re-layouts: 10.5 us -> 3.98 us
    pallas_call x0 -> x2, Pallas kernels: none -> 67.1 us  [the longest x1 35.3 us: gather_call(): pl.pallas_call(functools.partial(gather_kernel, wide), out_shape=jax.Shap...]
    reduce_scatter x1 -> x0, waiting for transfers between devices: 63.6 us -> none  [local(): mixed = lax.psum_scatter(summed, 'wide', scatter_dimension=0, tiled=True)]
    unnamed x6 -> x0, waiting for transfers between devices: 61.8 us -> none
    all_gather x1 -> x0, blocking collectives: 32 us -> none  [local(): column = lax.all_gather(hidden, 'wide', axis=0, tiled=True)]
    unnamed x14 -> x15, local copies, waits for them, and re-layouts: 9.15 us -> 3.33 us
    dot_general x1, matrix products: 10.3 us -> 6.91 us  [local(): jnp.einsum('rd,shd->rsh', normed, w_in[:, 1], preferred_element_type=jnp....]
    dot_general x2 -> x1, matrix products: 3.12 us -> 0.17 us  [local(): jnp.dot(order, attn_heads, preferred_element_type=jnp.float32)]
  transfers between devices with their start and end apart: 4 -> 0, of which waited for: 3 -> 0; matrix products, arithmetic and copies ran while one was open for 0% -> 0% of each run, Pallas kernels for 0% -> 0%
where the time goes in v2:
time: 134 us
  Pallas kernels  67.1 us (50%)
  blocking collectives  32.3 us (24%)
  matrix products  24.9 us (19%)
  other arithmetic  5.69 us (4%)
  local copies, waits for them, and re-layouts  3.98 us (3%)
    pallas_call x1, Pallas kernels, gather_call(): pl.pallas_call(functools.partial(gather_kernel, wide), out_shape=jax.Shap...  35.3 us
    all_gather x1, blocking collectives, local(): metas = lax.all_gather(meta, 'wide', axis=0, tiled=True)  32.3 us
    pallas_call x1, Pallas kernels, scatter_call(): pl.pallas_call(functools.partial(scatter_kernel, wide), out_shape=jax.Sha...  31.8 us
    dot_general x1, matrix products, local(): jnp.dot(act.reshape(wide * rows, slot_local * hid), w_down.reshape(slot_l...  16.8 us
    dot_general x1, matrix products, local(): jnp.einsum('rd,shd->rsh', normed, w_in[:, 1], preferred_element_type=jnp....  6.91 us
    unnamed x15, local copies, waits for them, and re-layouts  3.33 us

profile of v2, /device:TPU:0, one launch (start us, length us, event | category | flops | bytes accessed | tf_op | source)
XLA Modules:
  0.0 134.2 jit_solution(5110952912911438836)
XLA Ops:
  0.0 0.0 copy-start
  0.0 0.9 fusion.21
  0.9 0.7 broadcast_select_fusion
  1.6 0.1 dynamic-slice_convert_fusion
  1.7 0.7 fusion.23
  2.3 0.2 convert_reduce_fusion
  2.5 0.7 convert_element_type.53
  3.2 0.7 pad_maximum_fusion
  3.9 0.2 select_reduce_fusion
  4.2 32.3 %all_gather.3 = f32[1024,9]{0,1:T(8,128)S(1)} all-gather(f32[128,9]{0,1:T(8,128)S(1)} %select_reduce_fusion), channel_id=1, replica_groups=mesh['wide'=8,'narrow'=4] {'wide'}, dimensions={0}, use_global_device_ids=true | all-gather | bytes 41472 | tf_op jit(solution)/shard_map/all_gather | solution.py:347
  36.4 0.0 copy-done
  36.4 0.2 convolution_convert_fusion.attn_ref
  36.6 1.1 fusion.17.res_ref
  37.7 0.0 copy-start.3
  37.7 0.1 reshape.81
  37.8 0.1 copy.29
  37.9 0.2 reshape.82
  38.1 0.1 select_reduce_fusion.1
  38.2 0.0 copy-start.1
  38.2 1.3 copy-done.1
  39.5 0.0 slice-start
  39.5 35.3 %shard_map.100 = bf16[1024,1536]{1,0:T(8,128)(2,1)S(1)} custom-call(bf16[128,384]{1,0:T(8,128)(2,1)S(1)} %convolution_convert_fusion.attn_ref, bf16[384,1536]{1,0:T(8,128)(2,1)S(1)} %copy-done.1, f32[128,384]{1,0:T(8,128)S(1)} %fusion.17.res_ref), custom_call_target="tpu_custom_call" | custom-call | tf_op jit(solution)/shard_map/pallas_call | solution.py:147
  74.9 0.0 slice-start.1
  74.9 0.7 fusion
  75.6 0.0 copy-done.3
  75.6 0.0 slice-start.2
  75.6 0.8 fusion.2
  76.4 0.0 copy-start.2
  76.4 0.3 copy.26
  76.7 1.4 %copy-done.2 = bf16[8,8,16,1536]{3,2,1,0:T(8,128)(2,1)} copy-done((bf16[8,8,16,1536]{3,2,1,0:T(8,128)(2,1)}, bf16[8,8,16,1536]{3,2,1,0:T(8,128)(2,1)S(1)}, u32[]{:S(2)}) %copy-start.2) | copy-done | bytes 3145752
  78.1 0.0 slice-done
  78.1 0.0 slice-done.1
  78.1 0.0 slice-done.2
  78.1 6.9 %fusion.3 = f32[1024,8,192]{0,2,1:T(8,128)} fusion(bf16[1024,1536,1]{1,0,2:T(8,128)(2,1)S(1)} %bitcast.46, bf16[8,2,192,1536]{3,2,1,0:T(8,128)(2,1)S(1)} %bitcast.50), kind=kOutput, calls=%fused_computation.7 | convolution fusion | flops 4831838208 | bytes 14155776 | tf_op jit(solution)/shard_map/rd,shd->rsh/dot_general | solution.py:375
  85.0 16.8 %bitcast_convert_fusion.low_ref = bf16[1024,1536]{1,0:T(8,128)(2,1)S(1)} fusion(bf16[8,192,1536]{2,1,0:T(8,128)(2,1)} %param.19, f32[1024,8,192]{0,2,1:T(8,128)} %fusion.3, bf16[1024,1536,1]{1,0,2:T(8,128)(2,1)} %bitcast.47, bf16[8,2,192,1536]{3,2,1,0:T(8,128)(2,1)} %param.18, f32[1024,8]{0,1:T(8,128)S(1)} %select_reduce_fusion.1), kind=kOutput, calls=%fused_computation.5 | convolution fusion | flops 9671540736 | bytes 22052864 | tf_op jit(solution)/shard_map/dot_general | solution.py:377
  101.7 31.8 %shard_map.101 = bf16[128,384]{1,0:T(8,128)(2,1)S(1)} custom-call(bf16[1024,1536]{1,0:T(8,128)(2,1)S(1)} %bitcast_convert_fusion.low_ref, bf16[128,384]{1,0:T(8,128)(2,1)S(1)} %dynamic_slice.10.base_ref, bf16[128,128]{1,0:T(8,128)(2,1)S(1)} %fusion.16.back_ref), custom_call_target="tpu_custom_call" | custom-call | tf_op jit(solution)/shard_map/pallas_call | solution.py:289
  133.5 0.6 copy.35
  (9 shorter events, 0.1 us)
Async XLA Ops:
  0.0 36.4 %copy-start = (bf16[128,384]{1,0:T(8,128)(2,1)S(1)}, bf16[128,384]{1,0:T(8,128)(2,1)}, u32[]{:S(2)}) copy-start(bf16[128,384]{1,0:T(8,128)(2,1)} %param.10) | copy-start | bytes 294916
  37.7 37.9 %copy-start.3 = (f32[1536]{0:T(1024)S(1)}, f32[1536]{0:T(1024)}, u32[]{:S(2)}) copy-start(f32[1536]{0:T(1024)} %param.13) | copy-start | bytes 18436
  38.2 1.3 copy-start.1
  39.5 38.6 %slice-start = ((s8[9437184]{0:T(1024)(128)(4,1)}), s8[4194304]{0:T(1024)(128)(4,1)S(1)}, s32[]{:S(2)}) async-start(s8[9437184]{0:T(1024)(128)(4,1)} %bitcast.49), calls=%async_computation | async-start | bytes 8388608
  74.9 3.2 %slice-start.1 = ((s8[9437184]{0:T(1024)(128)(4,1)}), s8[4194304]{0:T(1024)(128)(4,1)S(1)}, s32[]{:S(2)}) async-start(s8[9437184]{0:T(1024)(128)(4,1)} %bitcast.49), calls=%async_computation.1 | async-start | bytes 8388608
  75.6 2.5 %slice-start.2 = ((s8[9437184]{0:T(1024)(128)(4,1)}), s8[1048576]{0:T(1024)(128)(4,1)S(1)}, s32[]{:S(2)}) async-start(s8[9437184]{0:T(1024)(128)(4,1)} %bitcast.49), calls=%async_computation.2 | async-start | bytes 2097152
  76.4 1.7 %copy-start.2 = (bf16[8,8,16,1536]{3,2,1,0:T(8,128)(2,1)}, bf16[8,8,16,1536]{3,2,1,0:T(8,128)(2,1)S(1)}, u32[]{:S(2)}) copy-start(bf16[8,8,16,1536]{3,2,1,0:T(8,128)(2,1)S(1)} %fusion.2) | copy-start | bytes 9437188

commit v3 on v2

--- a/solution.py
+++ b/solution.py
@@ -42,7 +42,9 @@
     attn_ref,
     w_ref,
     res_ref,
+    meta_ref,
     out_ref,
+    metas_ref,
     parts,
     got,
     mine,
@@ -55,6 +57,8 @@
     y_recv,
     core_send,
     core_recv,
+    meta_send,
+    meta_recv,
 ):
     me, col = lax.axis_index("wide"), lax.axis_index("narrow")
     half, core = col // 2, lax.rem(col, 2)
@@ -62,6 +66,23 @@
     core_col = half * 2 + 1 - core
     rows, cols = res_ref.shape
     greet(wide, me, col, [lax.rem(col + k, NARROW) for k in range(1, NARROW)])
+
+    def meta_copy(j):
+        return remote(
+            meta_ref,
+            metas_ref.at[me],
+            meta_send.at[j],
+            meta_recv.at[j],
+            lax.rem(me + j, wide),
+            col,
+        )
+
+    def send_meta(j, carry):
+        meta_copy(j).start()
+        return carry
+
+    metas_ref[me] = meta_ref[...]
+    lax.fori_loop(1, wide, send_meta, 0)
 
     for p in range(NARROW):
         parts[p] = jnp.dot(
@@ -133,6 +154,7 @@
 
     def finish_wide(j, carry):
         wide_copy(j).wait_send()
+        meta_copy(j).wait()
         return carry
 
     lax.fori_loop(1, wide, finish_wide, 0)
@@ -140,15 +162,18 @@
         copy.wait_send()
 
 
-def gather_call(attn, w_out, res, wide):
+def gather_call(attn, w_out, res, meta, wide):
     rows, cols = res.shape
     dma = pltpu.SemaphoreType.DMA
     vmem = pl.BlockSpec(memory_space=pltpu.VMEM)
     return pl.pallas_call(
         functools.partial(gather_kernel, wide),
-        out_shape=jax.ShapeDtypeStruct((wide * rows, NARROW * cols), jnp.bfloat16),
-        in_specs=[vmem] * 3,
-        out_specs=pl.BlockSpec(memory_space=pl.ANY),
+        out_shape=(
+            jax.ShapeDtypeStruct((wide * rows, NARROW * cols), jnp.bfloat16),
+            jax.ShapeDtypeStruct((wide,) + meta.shape, jnp.float32),
+        ),
+        in_specs=[vmem] * 4,
+        out_specs=(pl.BlockSpec(memory_space=pl.ANY), vmem),
         scratch_shapes=[
             pltpu.VMEM((NARROW, rows, cols), jnp.bfloat16),
             pltpu.VMEM((NARROW - 1, rows, cols), jnp.bfloat16),
@@ -162,11 +187,13 @@
             dma((wide,)),
             dma((2, wide)),
             dma((2, wide)),
+            dma((wide,)),
+            dma((wide,)),
         ],
         compiler_params=pltpu.CompilerParams(
             collective_id=0, has_side_effects=True, vmem_limit_bytes=32 * 2**20
         ),
-    )(attn, w_out, res)
+    )(attn, w_out, res, meta)
 
 
 def scatter_kernel(
@@ -344,7 +371,8 @@
         axis=1,
     )
     meta = jnp.sum(jnp.where(perm[:, :, None], meta[None], 0.0), axis=1)
-    metas = lax.all_gather(meta, "wide", axis=0, tiled=True)
+    fields = meta.shape[1]
+    meta = jnp.pad(meta.T, ((0, -fields % 8), (0, 0)))
     attn = jnp.dot(order, attn_heads, preferred_element_type=jnp.float32).astype(jnp.bfloat16)
     res = jnp.dot(order, residual, preferred_element_type=jnp.float32)
 
@@ -355,8 +383,9 @@
             .reshape(wide * rows, x.shape[1])
         )
 
-    gathered = regroup(gather_call(attn, w_out, res, wide))
-    metas = regroup(metas)
+    gathered, metas = gather_call(attn, w_out, res, meta, wide)
+    gathered = regroup(gathered)
+    metas = regroup(metas[:, :fields].transpose(0, 2, 1).reshape(wide * rows, fields))
     whole = gathered.astype(jnp.float32)
     mean_sq = jnp.mean(whole * whole, axis=1, keepdims=True)
     normed = (whole * lax.rsqrt(mean_sq + 1e-06) * norm_gain).astype(jnp.bfloat16)

time: 134 us -> 111 us (0.83)
  blocking collectives: 32.3 us -> 0 us
  local copies, waits for them, and re-layouts: 3.98 us -> 8.47 us
  Pallas kernels: 67.1 us -> 70 us
  other arithmetic: 5.69 us -> 7.2 us
    all_gather x1 -> x0, blocking collectives: 32.3 us -> none  [local(): metas = lax.all_gather(meta, 'wide', axis=0, tiled=True)]
    pallas_call x1, Pallas kernels: 35.3 us -> 38.4 us  [gather_call(): pl.pallas_call(functools.partial(gather_kernel, wide), out_shape=(jax.Sha...]
    unnamed x15 -> x11, local copies, waits for them, and re-layouts: 3.33 us -> 4.74 us
where the time goes in v3:
time: 111 us
  Pallas kernels  70 us (63%)
  matrix products  24.9 us (22%)
  local copies, waits for them, and re-layouts  8.47 us (8%)
  other arithmetic  7.2 us (6%)
    pallas_call x1, Pallas kernels, gather_call(): pl.pallas_call(functools.partial(gather_kernel, wide), out_shape=(jax.Sha...  38.4 us
    pallas_call x1, Pallas kernels, scatter_call(): pl.pallas_call(functools.partial(scatter_kernel, wide), out_shape=jax.Sha...  31.7 us
    dot_general x1, matrix products, local(): jnp.dot(act.reshape(wide * rows, slot_local * hid), w_down.reshape(slot_l...  16.8 us
    dot_general x1, matrix products, local(): jnp.einsum('rd,shd->rsh', normed, w_in[:, 1], preferred_element_type=jnp....  6.89 us
    unnamed x11, local copies, waits for them, and re-layouts  4.74 us

profile of v3, /device:TPU:0, one launch (start us, length us, event | category | flops | bytes accessed | tf_op | source)
XLA Modules:
  0.0 110.8 jit_solution(10870300251487540781)
XLA Ops:
  0.0 0.0 copy-start
  0.0 0.0 copy-start.3
  0.0 0.9 fusion.21
  0.9 0.7 broadcast_select_fusion
  1.6 0.1 dynamic-slice_convert_fusion
  1.7 0.7 fusion.23
  2.3 0.2 convert_reduce_fusion
  2.5 0.7 convert_element_type.52
  3.2 0.7 pad_maximum_fusion
  3.9 0.2 select_reduce_fusion
  4.2 0.0 copy-done
  4.2 0.2 convolution_convert_fusion.attn_ref
  4.4 1.1 fusion.17.res_ref
  5.4 0.0 copy-start.1
  5.4 1.3 %copy-done.1 = bf16[384,1536]{1,0:T(8,128)(2,1)S(1)} copy-done((bf16[384,1536]{1,0:T(8,128)(2,1)S(1)}, bf16[384,1536]{1,0:T(8,128)(2,1)}, u32[]{:S(2)}) %copy-start.1) | copy-done | bytes 1179672
  6.7 38.4 %shard_map.100 = (bf16[1024,1536]{1,0:T(8,128)(2,1)S(1)}, f32[8,16,128]{2,1,0:T(8,128)S(1)}) custom-call(bf16[128,384]{1,0:T(8,128)(2,1)S(1)} %convolution_convert_fusion.attn_ref, bf16[384,1536]{1,0:T(8,128)(2,1)S(1)} %copy-done.1, f32[128,384]{1,0:T(8,128)S(1)} %fusion.17.res_ref, f32[16,128]{1,0:T(8,128)S(1)} %pad.4.meta_ref), custom_call_target="tpu_custom_call" | custom-call | tf_op jit(solution)/shard_map/pallas_call | solution.py:169
  45.1 0.6 copy.32
  45.7 0.7 fusion
  46.4 0.6 add_rsqrt_fusion
  47.0 0.9 reshape_reshape.3
  47.9 0.8 copy.33
  48.7 1.1 %reshape.78 = f32[1024,9]{0,1:T(8,128)S(1)} reshape(f32[8,8,16,9]{2,1,0,3:T(8,128)} %copy.33) | data formatting | bytes 73728 | tf_op jit(solution)/shard_map/reshape | solution.py:383
  49.8 0.1 select_reduce_fusion.1
  50.0 0.0 copy-done.3
  50.0 0.0 copy-start.4
  50.0 1.7 %fusion.2 = bf16[8,8,16,1536]{3,2,1,0:T(8,128)(2,1)S(1)} fusion(f32[1536]{0:T(1024)S(1)} %copy-done.3, f32[8,8,16]{2,1,0:T(8,128)} %add_rsqrt_fusion, bf16[1024,1536]{1,0:T(8,128)(2,1)S(1)} %get-tuple-element.7), kind=kLoop, calls=%fused_computation.4 | loop fusion | flops 6291456 | bytes 6301696 | tf_op jit(solution)/shard_map/convert_element_type | solution.py:391
  51.7 0.0 copy-start.2
  51.7 0.3 copy.29
  52.0 1.4 %copy-done.2 = bf16[8,8,16,1536]{3,2,1,0:T(8,128)(2,1)} copy-done((bf16[8,8,16,1536]{3,2,1,0:T(8,128)(2,1)}, bf16[8,8,16,1536]{3,2,1,0:T(8,128)(2,1)S(1)}, u32[]{:S(2)}) %copy-start.2) | copy-done | bytes 3145752
  53.4 1.4 %copy-done.4 = bf16[8,2,192,1536]{3,2,1,0:T(8,128)(2,1)S(1)} copy-done((bf16[8,2,192,1536]{3,2,1,0:T(8,128)(2,1)S(1)}, bf16[8,2,192,1536]{3,2,1,0:T(8,128)(2,1)}, u32[]{:S(2)}) %copy-start.4) | copy-done | bytes 9437208
  54.8 6.9 %fusion.3 = f32[1024,8,192]{0,2,1:T(8,128)} fusion(bf16[1024,1536,1]{1,0,2:T(8,128)(2,1)S(1)} %bitcast.49, bf16[8,2,192,1536]{3,2,1,0:T(8,128)(2,1)S(1)} %copy-done.4), kind=kOutput, calls=%fused_computation.7 | convolution fusion | flops 4831838208 | bytes 14155776 | tf_op jit(solution)/shard_map/rd,shd->rsh/dot_general | solution.py:404
  61.7 16.8 %bitcast_convert_fusion.low_ref = bf16[1024,1536]{1,0:T(8,128)(2,1)S(1)} fusion(bf16[8,192,1536]{2,1,0:T(8,128)(2,1)} %param.19, f32[1024,8,192]{0,2,1:T(8,128)} %fusion.3, bf16[1024,1536,1]{1,0,2:T(8,128)(2,1)} %bitcast.50, bf16[8,2,192,1536]{3,2,1,0:T(8,128)(2,1)} %param.18, f32[1024,8]{0,1:T(8,128)S(1)} %select_reduce_fusion.1), kind=kOutput, calls=%fused_computation.5 | convolution fusion | flops 9671540736 | bytes 22052864 | tf_op jit(solution)/shard_map/dot_general | solution.py:406
  78.5 31.7 %shard_map.101 = bf16[128,384]{1,0:T(8,128)(2,1)S(1)} custom-call(bf16[1024,1536]{1,0:T(8,128)(2,1)S(1)} %bitcast_convert_fusion.low_ref, bf16[128,384]{1,0:T(8,128)(2,1)S(1)} %dynamic_slice.10.base_ref, bf16[128,128]{1,0:T(8,128)(2,1)S(1)} %fusion.16.back_ref), custom_call_target="tpu_custom_call" | custom-call | tf_op jit(solution)/shard_map/pallas_call | solution.py:316
  110.1 0.6 copy.39
  (9 shorter events, 0.1 us)
Async XLA Ops:
  0.0 4.2 %copy-start = (bf16[128,384]{1,0:T(8,128)(2,1)S(1)}, bf16[128,384]{1,0:T(8,128)(2,1)}, u32[]{:S(2)}) copy-start(bf16[128,384]{1,0:T(8,128)(2,1)} %param.10) | copy-start | bytes 294916
  0.0 50.0 %copy-start.3 = (f32[1536]{0:T(1024)S(1)}, f32[1536]{0:T(1024)}, u32[]{:S(2)}) copy-start(f32[1536]{0:T(1024)} %param.13) | copy-start | bytes 18436
  5.4 1.3 %copy-start.1 = (bf16[384,1536]{1,0:T(8,128)(2,1)S(1)}, bf16[384,1536]{1,0:T(8,128)(2,1)}, u32[]{:S(2)}) copy-start(bf16[384,1536]{1,0:T(8,128)(2,1)} %w_ref.1) | copy-start | bytes 3538948
  50.0 4.8 %copy-start.4 = (bf16[8,2,192,1536]{3,2,1,0:T(8,128)(2,1)S(1)}, bf16[8,2,192,1536]{3,2,1,0:T(8,128)(2,1)}, u32[]{:S(2)}) copy-start(bf16[8,2,192,1536]{3,2,1,0:T(8,128)(2,1)} %param.18) | copy-start | bytes 28311556
  51.7 1.7 %copy-start.2 = (bf16[8,8,16,1536]{3,2,1,0:T(8,128)(2,1)}, bf16[8,8,16,1536]{3,2,1,0:T(8,128)(2,1)S(1)}, u32[]{:S(2)}) copy-start(bf16[8,8,16,1536]{3,2,1,0:T(8,128)(2,1)S(1)} %fusion.2) | copy-start | bytes 9437188

commit v4 on v3

--- a/solution.py
+++ b/solution.py
@@ -20,6 +20,14 @@
         device_id=(wide_index, narrow_index),
         device_id_type=MESH,
     )
+
+
+def partner(me, j, wide):
+    out, bit = 0, 1
+    while bit < wide:
+        out = out + lax.rem(me // bit + j // bit, 2) * bit
+        bit *= 2
+    return out
 
 
 def greet(wide, me, col, others):
@@ -110,15 +118,15 @@
 
     def wide_copy(j):
         return remote(
-            mine, block(me, col), wide_send.at[j], wide_recv.at[j], lax.rem(me + j, wide), col
+            mine, block(me, col), wide_send.at[j], wide_recv.at[j], partner(me, j, wide), col
         )
 
     def y_copy(j):
-        b = block(lax.rem(me - j + wide, wide), col)
+        b = block(partner(me, j, wide), col)
         return remote(b, b, y_send.at[j], y_recv.at[j], me, y_col)
 
     def core_copy(j, h):
-        b = block(lax.rem(me - j + wide, wide), y_col if h else col)
+        b = block(partner(me, j, wide), y_col if h else col)
         return remote(b, b, core_send.at[h, j], core_recv.at[h, j], me, core_col)
 
     def send_wide(j, carry):
@@ -222,7 +230,7 @@
     greet(wide, me, col, [y_col, core_col])
 
     def target(j):
-        return lax.rem(me + 1 + j, wide)
+        return partner(me, wide - 1 - j, wide)
 
     def block(j, column):
         return low_ref.at[

time: 111 us -> 106 us (0.955)
  Pallas kernels: 70 us -> 64.4 us
    pallas_call x1, Pallas kernels: 31.7 us -> 28 us  [scatter_call(): pl.pallas_call(functools.partial(scatter_kernel, wide), out_shape=jax.Sha...]
    pallas_call x1, Pallas kernels: 38.4 us -> 36.4 us  [gather_call(): pl.pallas_call(functools.partial(gather_kernel, wide), out_shape=(jax.Sha...]
where the time goes in v4:
time: 106 us; the launch traced here: 105 us
  Pallas kernels  64.4 us (61%)
  matrix products  24.9 us (23%)
  local copies, waits for them, and re-layouts  8.47 us (8%)
  other arithmetic  7.2 us (7%)
    pallas_call x1, Pallas kernels, gather_call(): pl.pallas_call(functools.partial(gather_kernel, wide), out_shape=(jax.Sha...  36.4 us
    pallas_call x1, Pallas kernels, scatter_call(): pl.pallas_call(functools.partial(scatter_kernel, wide), out_shape=jax.Sha...  28 us
    dot_general x1, matrix products, local(): jnp.dot(act.reshape(wide * rows, slot_local * hid), w_down.reshape(slot_l...  16.8 us
    dot_general x1, matrix products, local(): jnp.einsum('rd,shd->rsh', normed, w_in[:, 1], preferred_element_type=jnp....  6.89 us
    unnamed x11, local copies, waits for them, and re-layouts  4.74 us

profile of v4, /device:TPU:0, one launch (start us, length us, event | category | flops | bytes accessed | tf_op | source)
XLA Modules:
  0.0 105.2 jit_solution(585527396997359308)
XLA Ops:
  0.0 0.0 copy-start
  0.0 0.0 copy-start.3
  0.0 0.9 fusion.21
  0.9 0.7 broadcast_select_fusion
  1.6 0.1 dynamic-slice_convert_fusion
  1.7 0.7 fusion.23
  2.3 0.2 convert_reduce_fusion
  2.5 0.7 convert_element_type.52
  3.2 0.7 pad_maximum_fusion
  3.9 0.2 select_reduce_fusion
  4.2 0.0 copy-done
  4.2 0.2 convolution_convert_fusion.attn_ref
  4.4 1.1 %fusion.17.res_ref = f32[128,384]{1,0:T(8,128)S(1)} fusion(bf16[128,384]{1,0:T(8,128)(2,1)} %param.12, s32[128]{0:T(128)S(1)} %multiply_add_fusion), kind=kOutput, calls=%fused_computation.25 | convolution fusion | flops 12599296 | bytes 295424 | tf_op jit(solution)/shard_map/dot_general | solution.py:385
  5.4 0.0 copy-start.1
  5.4 1.3 %copy-done.1 = bf16[384,1536]{1,0:T(8,128)(2,1)S(1)} copy-done((bf16[384,1536]{1,0:T(8,128)(2,1)S(1)}, bf16[384,1536]{1,0:T(8,128)(2,1)}, u32[]{:S(2)}) %copy-start.1) | copy-done | bytes 1179672
  6.7 36.4 %shard_map.100 = (bf16[1024,1536]{1,0:T(8,128)(2,1)S(1)}, f32[8,16,128]{2,1,0:T(8,128)S(1)}) custom-call(bf16[128,384]{1,0:T(8,128)(2,1)S(1)} %convolution_convert_fusion.attn_ref, bf16[384,1536]{1,0:T(8,128)(2,1)S(1)} %copy-done.1, f32[128,384]{1,0:T(8,128)S(1)} %fusion.17.res_ref, f32[16,128]{1,0:T(8,128)S(1)} %pad.4.meta_ref), custom_call_target="tpu_custom_call" | custom-call | tf_op jit(solution)/shard_map/pallas_call | solution.py:177
  43.1 0.6 copy.32
  43.8 0.7 fusion
  44.4 0.6 add_rsqrt_fusion
  45.1 0.9 reshape_reshape.3
  46.0 0.8 copy.33
  46.7 1.1 %reshape.78 = f32[1024,9]{0,1:T(8,128)S(1)} reshape(f32[8,8,16,9]{2,1,0,3:T(8,128)} %copy.33) | data formatting | bytes 73728 | tf_op jit(solution)/shard_map/reshape | solution.py:391
  47.9 0.1 select_reduce_fusion.1
  48.0 0.0 copy-done.3
  48.0 0.0 copy-start.4
  48.0 1.7 %fusion.2 = bf16[8,8,16,1536]{3,2,1,0:T(8,128)(2,1)S(1)} fusion(f32[1536]{0:T(1024)S(1)} %copy-done.3, f32[8,8,16]{2,1,0:T(8,128)} %add_rsqrt_fusion, bf16[1024,1536]{1,0:T(8,128)(2,1)S(1)} %get-tuple-element.7), kind=kLoop, calls=%fused_computation.4 | loop fusion | flops 6291456 | bytes 6301696 | tf_op jit(solution)/shard_map/convert_element_type | solution.py:399
  49.7 0.0 copy-start.2
  49.7 0.3 copy.29
  50.0 1.4 %copy-done.2 = bf16[8,8,16,1536]{3,2,1,0:T(8,128)(2,1)} copy-done((bf16[8,8,16,1536]{3,2,1,0:T(8,128)(2,1)}, bf16[8,8,16,1536]{3,2,1,0:T(8,128)(2,1)S(1)}, u32[]{:S(2)}) %copy-start.2) | copy-done | bytes 3145752
  51.4 1.4 %copy-done.4 = bf16[8,2,192,1536]{3,2,1,0:T(8,128)(2,1)S(1)} copy-done((bf16[8,2,192,1536]{3,2,1,0:T(8,128)(2,1)S(1)}, bf16[8,2,192,1536]{3,2,1,0:T(8,128)(2,1)}, u32[]{:S(2)}) %copy-start.4) | copy-done | bytes 9437208
  52.9 6.9 %fusion.3 = f32[1024,8,192]{0,2,1:T(8,128)} fusion(bf16[1024,1536,1]{1,0,2:T(8,128)(2,1)S(1)} %bitcast.49, bf16[8,2,192,1536]{3,2,1,0:T(8,128)(2,1)S(1)} %copy-done.4), kind=kOutput, calls=%fused_computation.7 | convolution fusion | flops 4831838208 | bytes 14155776 | tf_op jit(solution)/shard_map/rd,shd->rsh/dot_general | solution.py:412
  59.7 16.8 %bitcast_convert_fusion.low_ref = bf16[1024,1536]{1,0:T(8,128)(2,1)S(1)} fusion(bf16[8,192,1536]{2,1,0:T(8,128)(2,1)} %param.19, f32[1024,8,192]{0,2,1:T(8,128)} %fusion.3, bf16[1024,1536,1]{1,0,2:T(8,128)(2,1)} %bitcast.50, bf16[8,2,192,1536]{3,2,1,0:T(8,128)(2,1)} %param.18, f32[1024,8]{0,1:T(8,128)S(1)} %select_reduce_fusion.1), kind=kOutput, calls=%fused_computation.5 | convolution fusion | flops 9671540736 | bytes 22052864 | tf_op jit(solution)/shard_map/dot_general | solution.py:414
  76.5 28.0 %shard_map.101 = bf16[128,384]{1,0:T(8,128)(2,1)S(1)} custom-call(bf16[1024,1536]{1,0:T(8,128)(2,1)S(1)} %bitcast_convert_fusion.low_ref, bf16[128,384]{1,0:T(8,128)(2,1)S(1)} %dynamic_slice.10.base_ref, bf16[128,128]{1,0:T(8,128)(2,1)S(1)} %fusion.16.back_ref), custom_call_target="tpu_custom_call" | custom-call | tf_op jit(solution)/shard_map/pallas_call | solution.py:324
  104.5 0.6 copy.39
  (9 shorter events, 0.1 us)
Async XLA Ops:
  0.0 4.2 %copy-start = (bf16[128,384]{1,0:T(8,128)(2,1)S(1)}, bf16[128,384]{1,0:T(8,128)(2,1)}, u32[]{:S(2)}) copy-start(bf16[128,384]{1,0:T(8,128)(2,1)} %param.10) | copy-start | bytes 294916
  0.0 48.0 %copy-start.3 = (f32[1536]{0:T(1024)S(1)}, f32[1536]{0:T(1024)}, u32[]{:S(2)}) copy-start(f32[1536]{0:T(1024)} %param.13) | copy-start | bytes 18436
  5.4 1.3 %copy-start.1 = (bf16[384,1536]{1,0:T(8,128)(2,1)S(1)}, bf16[384,1536]{1,0:T(8,128)(2,1)}, u32[]{:S(2)}) copy-start(bf16[384,1536]{1,0:T(8,128)(2,1)} %w_ref.1) | copy-start | bytes 3538948
  48.0 4.8 %copy-start.4 = (bf16[8,2,192,1536]{3,2,1,0:T(8,128)(2,1)S(1)}, bf16[8,2,192,1536]{3,2,1,0:T(8,128)(2,1)}, u32[]{:S(2)}) copy-start(bf16[8,2,192,1536]{3,2,1,0:T(8,128)(2,1)} %param.18) | copy-start | bytes 28311556
  49.7 1.7 %copy-start.2 = (bf16[8,8,16,1536]{3,2,1,0:T(8,128)(2,1)}, bf16[8,8,16,1536]{3,2,1,0:T(8,128)(2,1)S(1)}, u32[]{:S(2)}) copy-start(bf16[8,8,16,1536]{3,2,1,0:T(8,128)(2,1)S(1)} %fusion.2) | copy-start | bytes 9437188
